TPU v7x, 32 devices: a whole 2x2x4 slice. The times are simulated.
32 devices in a mesh: band: 4 (over x, core), fft: 8 (over z, y).
Axes of the slice: x: 2, y: 2, z: 4, core: 2. Of those that a mesh axis runs over, the one named last changes fastest.
Arguments:
- valence_waves: bfloat16 [8, 96, 96, 96], P('band', 'fft'), may hold values from -6 to 6
- conduction_waves: bfloat16 [4, 96, 96, 96], P(None, 'fft'), may hold values from -6 to 6
- valence_energy: float32 [8], P('band'), may hold values from -1 to -0.1
- conduction_energy: float32 [4], replicated, may hold values from 0.1 to 1
- sphere_slots: int32 [16384], P('fft'), may hold values from 0 to 221183, as said below
Outputs:
- static_response: float32 [16384, 16384], P('fft', 'band')
Inputs may be any that keep to these rules, and one draw needn't show every extreme that they name: `sphere_slots`: entries g of one fft device's block (g // 2048 equal) are distinct; each block holds 0 and 221183.
All inputs are finite; a program needn't handle non-finite values.
Results may differ from a plain program's by a relative error of at most 0.009.
Values may be sent and summed in bfloat16 or wider, within the bound.
A program may use at most 320 MiB of HBM per device.

v0:
```python
import math

import jax
import jax.numpy as jnp
from jax import lax
from jax.sharding import PartitionSpec as P


def spread(block, axis, owner):
    block = jnp.where(lax.axis_index(axis) == owner, block, jnp.zeros_like(block))
    return lax.psum(block, axis)


def dft_tables(length):
    counter = jnp.arange(length, dtype=jnp.int32)
    product = counter[:, None] * counter[None, :] % length
    angles = product.astype(jnp.float32) * (2.0 * math.pi / length)
    factor = 1.0 / math.sqrt(length)
    return (
        (jnp.cos(angles) * factor).astype(jnp.bfloat16),
        (jnp.sin(angles) * factor).astype(jnp.bfloat16),
    )


def complex_pass(table_cos, table_sin, spectra, form):
    direct = jnp.einsum(form, table_cos, spectra, preferred_element_type=jnp.float32)
    swapped = jnp.einsum(form, table_sin, spectra, preferred_element_type=jnp.float32)
    half = spectra.shape[-1] // 2
    real_part = direct[..., :half] + swapped[..., half:]
    imag_part = direct[..., half:] - swapped[..., :half]
    return jnp.concatenate([real_part, imag_part], axis=-1)


def on_device(valence_waves, conduction_waves, valence_energy, conduction_energy, sphere_slots):
    length = conduction_waves.shape[2]
    bands = conduction_waves.shape[0]
    groups = lax.axis_size("band")
    pairs_all = groups * valence_waves.shape[0] * bands
    table_cos, table_sin = dft_tables(length)
    first_table = jnp.concatenate([table_cos, -table_sin], axis=1)
    blocks = []
    for vstep in range(valence_waves.shape[0]):
        density = valence_waves[vstep][None] * conduction_waves
        first_pass = jnp.einsum(
            "cxyz,zk->cxyk", density, first_table, preferred_element_type=jnp.float32
        ).astype(jnp.bfloat16)
        second_pass = complex_pass(table_cos, table_sin, first_pass, "ky,cxyq->cxkq").astype(
            jnp.bfloat16
        )
        piece = lax.all_to_all(second_pass, "fft", split_axis=2, concat_axis=1, tiled=True)
        third_pass = complex_pass(table_cos, table_sin, piece, "kx,cxyq->ckyq")
        elements = jnp.take(third_pass.reshape(piece.shape[0], -1), sphere_slots, axis=1)
        spacing = conduction_energy - valence_energy[vstep]
        factor = jnp.sqrt(4.0 / (spacing * pairs_all))
        blocks.append((factor[:, None] * elements).astype(jnp.bfloat16))
    scaled = jnp.concatenate(blocks, axis=0)
    contract = (((0,), (0,)), ((), ()))
    rows = lax.all_gather(scaled, "band", axis=0, tiled=True)
    ratio = lax.axis_size("fft") // groups
    first_root = lax.axis_index("band") * ratio
    slabs = []
    for slab_index in range(ratio):
        slabs.append(spread(rows, "fft", first_root + slab_index))
    owned = jnp.concatenate(slabs, axis=1)
    response = -lax.dot_general(rows, owned, contract, preferred_element_type=jnp.float32)
    return response


def solution(mesh):
    in_specs = (P("band", "fft", None, None), P(None, "fft", None, None), P("band"), P(), P("fft"))
    out_specs = P("fft", "band")
    return jax.shard_map(
        on_device, mesh=mesh, in_specs=in_specs, out_specs=out_specs, check_vma=False
    )
```

profile of v0, /device:TPU:24, one launch (start us, length us, event | category | flops | bytes accessed | tf_op | source)
XLA Modules:
  0.0 420.6 jit_solution(14117338957576890759)
XLA Ops:
  6.5 0.2 fusion.26
  6.7 0.0 copy-start.1
  6.8 0.2 multiply_convert_fusion.1
  7.0 0.0 copy-start.2
  7.0 1.8 slice_bitcast_fusion.1
  8.8 2.1 convolution_convert_fusion
  10.9 1.0 convolution_bitcast_fusion.2
  12.0 1.0 convolution_bitcast_fusion.3
  13.0 1.0 fusion.1
  14.0 0.7 pad_maximum_fusion.3
  14.7 3.8 copy.80
  18.5 6.2 %all-to-all-start.1 = ((bf16[4,12,96,192]{3,0,1,2:T(4,128)(2,1)}), bf16[4,12,96,192]{3,0,1,2:T(4,128)(2,1)S(1)}, u32[]{:S(2)}, u32[]{:S(2)}) async-start(bf16[4,12,96,192]{3,0,1,2:T(4,128)(2,1)} %copy.80), calls=%async_computation.1 | async-start | bytes 4718592 | tf_op jit(solution)/shard_map/all_to_all | solution.py:50
  24.7 1.8 convolution_convert_fusion.1
  26.5 1.0 convolution_bitcast_fusion.6
  27.6 1.0 convolution_bitcast_fusion.7
  28.6 1.0 fusion.3
  29.6 2.1 pad_maximum_fusion.2
  31.7 5.7 %copy.70 = bf16[4,12,96,192]{3,0,1,2:T(4,128)(2,1)} copy(bf16[4,12,96,192]{2,3,1,0:T(8,128)(2,1)} %pad_maximum_fusion.2) | data formatting | bytes 3538944 | tf_op jit(solution)/shard_map/concatenate | solution.py:31
  37.4 39.6 %all-to-all-done.1 = bf16[4,12,96,192]{3,0,1,2:T(4,128)(2,1)S(1)} async-done(((bf16[4,12,96,192]{3,0,1,2:T(4,128)(2,1)}), bf16[4,12,96,192]{3,0,1,2:T(4,128)(2,1)S(1)}, u32[]{:S(2)}, u32[]{:S(2)}) %all-to-all-start.1) | async-done | bytes 1769504 | tf_op jit(solution)/shard_map/all_to_all | solution.py:50
  77.0 5.8 %all-to-all-start = ((bf16[4,12,96,192]{3,0,1,2:T(4,128)(2,1)}), bf16[4,12,96,192]{3,0,1,2:T(4,128)(2,1)}, u32[]{:S(2)}, u32[]{:S(2)}) async-start(bf16[4,12,96,192]{3,0,1,2:T(4,128)(2,1)} %copy.70), calls=%async_computation | async-start | bytes 4718592 | tf_op jit(solution)/shard_map/all_to_all | solution.py:50
  82.8 0.0 all-reduce.3.cloned.1.call-start
  82.8 0.6 fusion.63
  83.4 1.3 divide_sqrt_fusion.1
  84.8 2.4 copy.82
  87.1 4.5 %copy.83 = bf16[4,96,12,192]{1,3,2,0:T(8,128)(2,1)S(1)} copy(bf16[4,96,12,192]{3,0,2,1:T(4,128)(2,1)} %bitcast.78) | data formatting | bytes 3538944 | tf_op jit(solution)/shard_map/all_to_all | solution.py:50
  91.7 3.1 convolution_bitcast_fusion
  94.8 3.1 convolution_bitcast_fusion.1
  97.9 36.9 %all-to-all-done = bf16[4,12,96,192]{3,0,1,2:T(4,128)(2,1)} async-done(((bf16[4,12,96,192]{3,0,1,2:T(4,128)(2,1)}), bf16[4,12,96,192]{3,0,1,2:T(4,128)(2,1)}, u32[]{:S(2)}, u32[]{:S(2)}) %all-to-all-start) | async-done | bytes 1769504 | tf_op jit(solution)/shard_map/all_to_all | solution.py:50
  134.8 4.0 copy.72
  138.8 4.5 %copy.73 = bf16[4,96,12,192]{1,3,2,0:T(8,128)(2,1)S(1)} copy(bf16[4,96,12,192]{3,0,2,1:T(4,128)(2,1)} %bitcast.79) | data formatting | bytes 3538944 | tf_op jit(solution)/shard_map/all_to_all | solution.py:50
  143.3 3.2 convolution_bitcast_fusion.4
  146.5 3.1 convolution_bitcast_fusion.5
  149.6 4.8 %slice_add_fusion = (f32[4,96,12,96]{1,3,2,0:T(8,128)S(1)}, f32[4,96,12,96]{1,3,2,0:T(8,128)S(1)}) fusion(f32[4,96,12,192]{1,3,2,0:T(8,128)} %convolution_bitcast_fusion, f32[4,96,12,192]{1,3,2,0:T(8,128)} %convolution_bitcast_fusion.1), kind=kLoop, calls=%fused_computation.6 | loop fusion | flops 884736 | bytes 10616832 | tf_op jit(solution)/shard_map/add | solution.py:29
  154.3 2.5 pad_maximum_fusion.1
  156.8 58.1 %copy.98 = f32[4,96,12,192]{0,3,2,1:T(8,128)} copy(f32[4,96,12,192]{1,3,2,0:T(8,128)} %pad_maximum_fusion.1) | data formatting | bytes 7077888 | tf_op jit(solution)/shard_map/reshape | solution.py:52
  215.0 20.5 %gather_fusion.1 = f32[2048,4]{1,0:T(8,128)S(1)} fusion(f32[4,221184]{0,1:T(8,128)} %bitcast.31, s32[2048]{0:T(1024)S(1)} %fusion.27), kind=kCustom, calls=%fused_computation.1.clone | custom fusion | bytes 73728 | tf_op jit(solution)/shard_map/jit(_take)/gather | solution.py:52
  235.5 0.3 copy.87
  235.8 4.8 %slice_add_fusion.2 = (f32[4,96,12,96]{1,3,2,0:T(8,128)S(1)}, f32[4,96,12,96]{1,3,2,0:T(8,128)S(1)}) fusion(f32[4,96,12,192]{1,3,2,0:T(8,128)} %convolution_bitcast_fusion.4, f32[4,96,12,192]{1,3,2,0:T(8,128)} %convolution_bitcast_fusion.5), kind=kLoop, calls=%fused_computation.12 | loop fusion | flops 884736 | bytes 10616832 | tf_op jit(solution)/shard_map/add | solution.py:29
  240.6 2.6 pad_maximum_fusion
  243.2 58.1 %copy.96 = f32[4,96,12,192]{0,3,2,1:T(8,128)} copy(f32[4,96,12,192]{1,3,2,0:T(8,128)} %pad_maximum_fusion) | data formatting | bytes 7077888 | tf_op jit(solution)/shard_map/reshape | solution.py:52
  301.3 20.5 %gather_fusion = f32[2048,4]{1,0:T(8,128)S(1)} fusion(f32[4,221184]{0,1:T(8,128)} %bitcast.17, s32[2048]{0:T(1024)S(1)} %fusion.27), kind=kCustom, calls=%fused_computation.clone | custom fusion | bytes 73728 | tf_op jit(solution)/shard_map/jit(_take)/gather | solution.py:52
  321.9 0.3 copy.77
  322.2 0.1 fusion.17
  322.3 5.6 %all_gather.3 = bf16[32,2048]{1,0:T(8,128)(2,1)S(1)} all-gather(bf16[8,2048]{1,0:T(8,128)(2,1)S(1)} %pad_maximum_fusion.4), channel_id=1, replica_groups=mesh['band'=4,'fft'=8] {'band'}, dimensions={0}, use_global_device_ids=true | all-gather | bytes 163840 | tf_op jit(solution)/shard_map/all_gather | solution.py:58
  328.0 0.7 broadcast_select_fusion.1
  328.7 0.0 all-reduce.3.cloned.1.call-update
  328.7 70.1 %all-reduce.3.cloned.1.call-done = (bf16[32,2048]{1,0:T(8,128)(2,1)}, bf16[32,2048]{1,0:T(8,128)(2,1)}) async-done(((bf16[32,2048]{1,0:T(8,128)(2,1)}, bf16[32,2048]{1,0:T(8,128)(2,1)}), (bf16[32,2048]{1,0:T(8,128)(2,1)}, bf16[32,2048]{1,0:T(8,128)(2,1)})) %all-reduce.3.cloned.1.call-update) | async-done | bytes 262160 | tf_op jit(solution)/shard_map/psum | solution.py:11
  398.8 15.0 %convolution_negate_fusion = f32[2048,4096]{1,0:T(8,128)} fusion(bf16[32,2048]{1,0:T(8,128)(2,1)S(1)} %all_gather.3, bf16[32,2048]{1,0:T(8,128)(2,1)} %get-tuple-element.6, bf16[32,2048]{1,0:T(8,128)(2,1)} %get-tuple-element.7), kind=kOutput, calls=%fused_computation.2 | convolution fusion | flops 545783808 | bytes 33947648 | tf_op jit(solution)/shard_map/dot_general | solution.py:65
  (13 shorter events, 0.1 us)
Async XLA Ops:
  6.7 4.2 copy-start.1
  7.0 3.9 copy-start.2
  18.5 6.2 %copy-start = (bf16[4,12,96,96]{3,2,1,0:T(8,128)(2,1)S(1)}, bf16[4,12,96,96]{3,2,1,0:T(8,128)(2,1)}, u32[]{:S(2)}) copy-start(bf16[4,12,96,96]{3,2,1,0:T(8,128)(2,1)} %param.8) | copy-start | bytes 2654212
  18.5 58.5 %all-to-all-start.1 = ((bf16[4,12,96,192]{3,0,1,2:T(4,128)(2,1)}), bf16[4,12,96,192]{3,0,1,2:T(4,128)(2,1)S(1)}, u32[]{:S(2)}, u32[]{:S(2)}) async-start(bf16[4,12,96,192]{3,0,1,2:T(4,128)(2,1)} %copy.80), calls=%async_computation.1 | async-start | bytes 4718592 | tf_op jit(solution)/shard_map/all_to_all | solution.py:50
  37.4 45.4 %copy-start.4 = (f32[2]{0:T(128)S(1)}, f32[2]{0:T(128)}, u32[]{:S(2)}) copy-start(f32[2]{0:T(128)} %param.9) | copy-start | bytes 28
  37.4 46.0 %copy-start.5 = (f32[4]{0:T(128)S(1)}, f32[4]{0:T(128)}, u32[]{:S(2)}) copy-start(f32[4]{0:T(128)} %param.10) | copy-start | bytes 52
  37.4 47.3 %copy-start.3 = (s32[2048]{0:T(1024)S(1)}, s32[2048]{0:T(1024)}, u32[]{:S(2)}) copy-start(s32[2048]{0:T(1024)} %param.11) | copy-start | bytes 24580
  77.0 57.8 %all-to-all-start = ((bf16[4,12,96,192]{3,0,1,2:T(4,128)(2,1)}), bf16[4,12,96,192]{3,0,1,2:T(4,128)(2,1)}, u32[]{:S(2)}, u32[]{:S(2)}) async-start(bf16[4,12,96,192]{3,0,1,2:T(4,128)(2,1)} %copy.70), calls=%async_computation | async-start | bytes 4718592 | tf_op jit(solution)/shard_map/all_to_all | solution.py:50
  82.8 315.9 %all-reduce.3.cloned.1.call-start = ((), (), s32[]{:S(2)}) async-start(), calls=%async_computation.2 | async-start | bytes 524288 | tf_op jit(solution)/shard_map/psum | solution.py:11
Sparse Core Ops, SparseCore 0:
  328.8 69.8 all-reduce.2
where the time goes:
time: 425 us; the launch traced here: 421 us
  local copies, waits for them, and re-layouts  185 us (44%)
  waiting for transfers between devices  147 us (35%)
  matrix products  35.5 us (8%)
  other arithmetic  21.9 us (5%)
  between operations  13.6 us (3%)
  starting transfers between devices  12 us (3%)
  blocking collectives  5.65 us (1%)
    reshape x2, local copies, waits for them, and re-layouts, on_device(): third_pass.reshape(piece.shape[0], -1)  116 us
    all_to_all x2, waiting for transfers between devices, on_device(): lax.all_to_all(second_pass, 'fft', split_axis=2, concat_axis=1, tiled=True)  76.4 us
    psum x1, waiting for transfers between devices, spread(): return lax.psum(block, axis)  70.1 us
    gather x4, local copies, waits for them, and re-layouts, on_device(): jnp.take(third_pass.reshape(piece.shape[0], -1), sphere_slots, axis=1)  41.7 us
    all_to_all x4, local copies, waits for them, and re-layouts, on_device(): lax.all_to_all(second_pass, 'fft', split_axis=2, concat_axis=1, tiled=True)  15.4 us
    dot_general x1, matrix products, on_device(): lax.dot_general(rows, owned, contract, preferred_element_type=jnp.float32)  15 us
    all_to_all x2, starting transfers between devices, on_device(): lax.all_to_all(second_pass, 'fft', split_axis=2, concat_axis=1, tiled=True)  12 us
    concatenate x2, local copies, waits for them, and re-layouts, complex_pass(): return jnp.concatenate([real_part, imag_part], axis=-1)  9.57 us
  transfers between devices with their start and end apart: 3, of which 3 were waited for; matrix products, arithmetic and copies ran while one was open for 7% of the time, Pallas kernels for 0%

commit v1 on v0

v1 whole, which is shorter than its diff:
```python
import functools
import math

import jax
import jax.numpy as jnp
from jax import lax
from jax.experimental import pallas as pl
from jax.experimental.pallas import tpu as pltpu
from jax.sharding import PartitionSpec as P

LANES = 128


def dft_tables(length):
    counter = jnp.arange(length, dtype=jnp.int32)
    product = counter[:, None] * counter[None, :] % length
    angles = product.astype(jnp.float32) * (2.0 * math.pi / length)
    factor = 1.0 / math.sqrt(length)
    return (
        (jnp.cos(angles) * factor).astype(jnp.bfloat16),
        (jnp.sin(angles) * factor).astype(jnp.bfloat16),
    )


def transform(valence_ref, conduction_ref, first_ref, second_ref, planes, length):
    bands = conduction_ref.shape[0]
    pairs = valence_ref.shape[0] * bands
    slab = valence_ref.shape[1]

    def one_plane(x, carry):
        for v in range(valence_ref.shape[0]):
            density = (valence_ref[v, x][None] * conduction_ref[:, x]).reshape(bands * length, length)
            first = jnp.dot(density, first_ref[...], preferred_element_type=jnp.float32)
            first = first.astype(jnp.bfloat16)
            for c in range(0, bands, 2):
                columns = []
                for d in range(c, c + 2):
                    one = first[d * length : (d + 1) * length]
                    columns.append(jnp.concatenate([one[:, :LANES], one[:, LANES:]], axis=0))
                both = jnp.concatenate(columns, axis=1)
                second = jnp.dot(second_ref[...], both, preferred_element_type=jnp.float32)
                for d in range(2):
                    row = x * pairs + v * bands + c + d
                    planes[pl.ds(row, 2 * length, stride=slab * pairs), :] = second[
                        :, d * LANES : (d + 1) * LANES
                    ]
        return carry

    lax.fori_loop(0, slab, one_plane, 0)


def sample_tile(codes, left, xtable_ref, pairs, slab):
    tile = codes.shape[1]
    depth = left.shape[1]
    kx = codes & 255
    column = (codes >> 8) & 4095
    imag = (codes >> 20) > 0
    hot = lax.broadcasted_iota(jnp.int32, (depth, tile), 0) == column
    hot = jnp.where(hot, 1.0, 0.0).astype(jnp.bfloat16)
    picked = jnp.dot(left[...], hot, preferred_element_type=jnp.float32)
    hot_x = lax.broadcasted_iota(jnp.int32, (LANES, tile), 0) == kx
    hot_x = jnp.where(hot_x, 1.0, 0.0).astype(jnp.bfloat16)
    waves = jnp.dot(xtable_ref[...], hot_x, preferred_element_type=jnp.float32)
    half = waves.shape[0] // 2
    cos, sin = waves[:half], waves[half:]
    with_re = jnp.where(imag, -sin, cos)
    with_im = jnp.where(imag, cos, sin)
    total = jnp.zeros((pairs, tile), jnp.float32)
    for x in range(slab):
        re = picked[x * pairs : (x + 1) * pairs]
        im = picked[(slab + x) * pairs : (slab + x + 1) * pairs]
        total += with_re[x : x + 1] * re + with_im[x : x + 1] * im
    return total


def elements_kernel(length, owners, tile, codes_ref, valence_ref, conduction_ref, first_ref,
                    second_ref, xtable_ref, out_ref, planes, left):
    pairs = valence_ref.shape[0] * conduction_ref.shape[0]
    slab = valence_ref.shape[1]
    rows = 2 * slab * pairs
    own = codes_ref.shape[1] // owners
    yslab = length // owners
    transform(valence_ref, conduction_ref, first_ref, second_ref, planes, length)

    def one_owner(o, carry):
        for k in range(yslab):
            part = planes[pl.ds(pl.multiple_of((o * yslab + k) * rows, rows), rows), :]
            left[:, k * LANES : (k + 1) * LANES] = part.astype(jnp.bfloat16)

        def one_tile(t, carry):
            at = pl.ds(pl.multiple_of(o * own + t * tile, tile), tile)
            out_ref[:, at] = sample_tile(codes_ref[:, at], left, xtable_ref, pairs, slab)
            return carry

        return lax.fori_loop(0, own // tile, one_tile, carry)

    lax.fori_loop(0, owners, one_owner, 0)


def on_device(valence_waves, conduction_waves, valence_energy, conduction_energy, sphere_slots):
    length = conduction_waves.shape[2]
    bands = conduction_waves.shape[0]
    slab = conduction_waves.shape[1]
    groups = lax.axis_size("band")
    owners = lax.axis_size("fft")
    pairs = valence_waves.shape[0] * bands
    pairs_all = groups * pairs
    own = sphere_slots.shape[0]
    yslab = length // owners
    me = lax.axis_index("fft")

    table_cos, table_sin = dft_tables(length)
    gap = ((0, 0), (0, LANES - length))
    first_table = jnp.concatenate([jnp.pad(table_cos, gap), jnp.pad(-table_sin, gap)], axis=1)
    second_table = jnp.stack(
        [
            jnp.concatenate([table_cos, table_sin], axis=1),
            jnp.concatenate([-table_sin, table_cos], axis=1),
        ],
        axis=1,
    ).reshape(2 * length, 2 * length)
    short = -slab % 16
    pieces = []
    for table in (table_cos, table_sin):
        piece = lax.dynamic_slice_in_dim(table, me * slab, slab, axis=0)
        pieces.append(jnp.pad(piece, ((0, short), (0, LANES - length))))
    xtable = jnp.concatenate(pieces, axis=0)

    width = 2 * length
    kx = sphere_slots // (yslab * width)
    ky = (sphere_slots // width) % yslab
    comp = sphere_slots % width
    imag = (comp >= length).astype(jnp.int32)
    codes = kx + ((ky * LANES + comp - imag * length) << 8) + (imag << 20)
    codes = lax.all_gather(codes, "fft", axis=0, tiled=True)[None]

    partial = pl.pallas_call(
        functools.partial(elements_kernel, length, owners, min(512, own)),
        out_shape=jax.ShapeDtypeStruct((pairs, owners * own), jnp.float32),
        in_specs=[pl.BlockSpec(memory_space=pltpu.VMEM)] * 6,
        out_specs=pl.BlockSpec(memory_space=pltpu.VMEM),
        scratch_shapes=[
            pltpu.VMEM((2 * length * slab * pairs, LANES), jnp.float32),
            pltpu.VMEM((2 * slab * pairs, yslab * LANES), jnp.bfloat16),
        ],
        compiler_params=pltpu.CompilerParams(vmem_limit_bytes=48 * 2**20),
        name="elements",
    )(codes, valence_waves, conduction_waves, first_table, second_table, xtable)
    elements = lax.psum_scatter(partial, "fft", scatter_dimension=1, tiled=True)
    spacing = conduction_energy[None, :] - valence_energy[:, None]
    factor = jnp.sqrt(4.0 / (spacing * pairs_all)).reshape(pairs)
    scaled = (factor[:, None] * elements).astype(jnp.bfloat16)

    rows = lax.all_gather(scaled, "band", axis=0, tiled=True)
    whole = lax.all_gather(rows, "fft", axis=1, tiled=True)
    share = owners * own // groups
    owned = lax.dynamic_slice_in_dim(whole, lax.axis_index("band") * share, share, axis=1)
    contract = (((0,), (0,)), ((), ()))
    return -lax.dot_general(rows, owned, contract, preferred_element_type=jnp.float32)


def solution(mesh):
    in_specs = (P("band", "fft", None, None), P(None, "fft", None, None), P("band"), P(), P("fft"))
    out_specs = P("fft", "band")
    return jax.shard_map(
        on_device, mesh=mesh, in_specs=in_specs, out_specs=out_specs, check_vma=False
    )
```

time: 425 us -> 206 us (0.48)
  local copies, waits for them, and re-layouts: 185 us -> 2.63 us
  waiting for transfers between devices: 147 us -> 103 us
  Pallas kernels: 0 us -> 28.9 us
  blocking collectives: 5.65 us -> 33.7 us
  other arithmetic: 21.9 us -> 3.16 us
  matrix products: 35.5 us -> 17.3 us
  starting transfers between devices: 12 us -> 0.04 us
    reshape x2 -> x1, local copies, waits for them, and re-layouts: 116 us -> 0.1 us  [on_device(): second_table = jnp.stack([jnp.concatenate([table_cos, table_sin], axis=1)...]
    all_to_all x2 -> x0, waiting for transfers between devices: 76.4 us -> none  [on_device(): lax.all_to_all(second_pass, 'fft', split_axis=2, concat_axis=1, tiled=True)]
    psum x1 -> x0, waiting for transfers between devices: 70.1 us -> none  [spread(): return lax.psum(block, axis)]
    reduce_scatter x0 -> x1, waiting for transfers between devices: none -> 64.2 us  [on_device(): elements = lax.psum_scatter(partial, 'fft', scatter_dimension=1, tiled=True)]
    gather x4 -> x0, local copies, waits for them, and re-layouts: 41.7 us -> none  [on_device(): jnp.take(third_pass.reshape(piece.shape[0], -1), sphere_slots, axis=1)]
    all_gather x0 -> x1, waiting for transfers between devices: none -> 39.2 us  [on_device(): whole = lax.all_gather(rows, 'fft', axis=1, tiled=True)]
    pallas_call x0 -> x1, Pallas kernels: none -> 28.9 us  [on_device(): pl.pallas_call(functools.partial(elements_kernel, length, owners, min(512...]
    all_gather x0 -> x1, blocking collectives: none -> 27.8 us  [on_device(): codes = lax.all_gather(codes, 'fft', axis=0, tiled=True)[None]]
  transfers between devices with their start and end apart: 3 -> 2, of which waited for: 3 -> 2; matrix products, arithmetic and copies ran while one was open for 7% -> 0% of each run, Pallas kernels for 0% -> 0%
where the time goes in v1:
time: 206 us; the launch traced here: 203 us
  waiting for transfers between devices  103 us (50%)
  blocking collectives  33.7 us (16%)
  Pallas kernels  28.9 us (14%)
  matrix products  17.3 us (8%)
  between operations  13.5 us (7%)
  other arithmetic  3.16 us (2%)
  local copies, waits for them, and re-layouts  2.63 us (1%)
    reduce_scatter x1, waiting for transfers between devices, on_device(): elements = lax.psum_scatter(partial, 'fft', scatter_dimension=1, tiled=True)  64.2 us
    all_gather x1, waiting for transfers between devices, on_device(): whole = lax.all_gather(rows, 'fft', axis=1, tiled=True)  39.2 us
    pallas_call x1, Pallas kernels, on_device(): pl.pallas_call(functools.partial(elements_kernel, length, owners, min(512...  28.9 us
    all_gather x1, blocking collectives, on_device(): codes = lax.all_gather(codes, 'fft', axis=0, tiled=True)[None]  27.8 us
    dot_general x1, matrix products, on_device(): lax.dot_general(rows, owned, contract, preferred_element_type=jnp.float32)  17.3 us
    all_gather x1, blocking collectives, on_device(): rows = lax.all_gather(scaled, 'band', axis=0, tiled=True)  5.86 us
  transfers between devices with their start and end apart: 2, of which 2 were waited for; matrix products, arithmetic and copies ran while one was open for 0% of the time, Pallas kernels for 0%

profile of v1, /device:TPU:24, one launch (start us, length us, event | category | flops | bytes accessed | tf_op | source)
XLA Modules:
  0.0 202.6 jit_solution(5351509844367045897)
XLA Ops:
  6.5 0.0 reduce-scatter.2.cloned.1.call-start
  6.5 0.2 multiply_convert_fusion.2
  6.7 0.2 fusion.11
  7.0 0.2 multiply_convert_fusion.1
  7.2 0.7 fusion.13
  7.9 0.1 maximum_bitcast_fusion
  8.1 0.1 copy.7
  8.2 0.1 reshape.27.second_ref
  8.3 27.8 %all_gather.9 = s32[16384]{0:T(1024)S(1)} all-gather(s32[2048]{0:T(1024)S(1)} %fusion.13), channel_id=1, replica_groups=mesh['band'=4,'fft'=8] {'fft'}, dimensions={0}, use_global_device_ids=true | all-gather | bytes 73728 | tf_op jit(solution)/shard_map/all_gather | solution.py:135
  36.1 0.0 copy-start
  36.1 1.3 copy-done
  37.4 0.0 copy-start.1
  37.4 1.1 copy-done.1
  38.5 28.9 %elements.1 = f32[8,16384]{1,0:T(8,128)} custom-call(s32[1,16384]{1,0:T(1,128)S(1)} %bitcast.6, bf16[2,12,96,96]{3,2,1,0:T(8,128)(2,1)S(1)} %copy-done.1, bf16[4,12,96,96]{3,2,1,0:T(8,128)(2,1)S(1)} %copy-done, bf16[96,256]{1,0:T(8,128)(2,1)S(1)} %fusion.5.first_ref, bf16[192,192]{1,0:T(8,128)(2,1)S(1)} %reshape.27.second_ref, ...), custom_call_target="tpu_custom_call" | custom-call | tf_op jit(solution)/shard_map/elements/pallas_call | solution.py:137
  67.4 0.0 reduce-scatter.2.cloned.1.call-update
  67.4 0.0 all-gather.2.cloned.1.call-start
  67.5 0.8 divide_sqrt_fusion
  68.2 0.1 sqrt.11
  68.3 64.2 %reduce-scatter.2.cloned.1.call-done = f32[8,2048]{1,0:T(8,128)} async-done(((f32[8,16384]{1,0:T(8,128)}), f32[8,2048]{1,0:T(8,128)}) %reduce-scatter.2.cloned.1.call-update) | async-done | bytes 65552 | tf_op jit(solution)/shard_map/reduce_scatter | solution.py:149
  132.5 0.9 multiply_convert_fusion
  133.4 5.9 %all_gather.10 = bf16[32,2048]{1,0:T(8,128)(2,1)} all-gather(bf16[8,2048]{1,0:T(8,128)(2,1)S(1)} %multiply_convert_fusion), channel_id=1, replica_groups=mesh['band'=4,'fft'=8] {'band'}, dimensions={0}, use_global_device_ids=true | all-gather | bytes 163840 | tf_op jit(solution)/shard_map/all_gather | solution.py:154
  139.3 0.0 all-gather.2.cloned.1.call-update
  139.3 39.2 %all-gather.2.cloned.1.call-done = bf16[32,16384]{1,0:T(8,128)(2,1)} async-done(((bf16[32,2048]{1,0:T(8,128)(2,1)}), bf16[32,16384]{1,0:T(8,128)(2,1)}) %all-gather.2.cloned.1.call-update) | async-done | bytes 1048592 | tf_op jit(solution)/shard_map/all_gather | solution.py:155
  178.5 17.3 %convolution_negate_fusion = f32[2048,4096]{1,0:T(8,128)} fusion(bf16[32,2048]{1,0:T(8,128)(2,1)} %all_gather.10, bf16[32,16384]{1,0:T(8,128)(2,1)} %all-gather.2.cloned.1.call-done, s32[]{:T(128)S(6)} %select_n.52), kind=kOutput, calls=%fused_computation | convolution fusion | flops 545259520 | bytes 33947652 | tf_op jit(solution)/shard_map/dot_general | solution.py:159
  (4 shorter events, 0.1 us)
Async XLA Ops:
  6.5 126.0 %reduce-scatter.2.cloned.1.call-start = ((), (), s32[]{:S(2)}) async-start(), calls=%async_computation.1 | async-start | bytes 589824 | tf_op jit(solution)/shard_map/reduce_scatter | solution.py:149
  36.1 1.3 copy-start
  37.4 1.1 copy-start.1
  67.4 111.1 %all-gather.2.cloned.1.call-start = ((), (), s32[]{:S(2)}) async-start(), calls=%async_computation.2 | async-start | bytes 1179648 | tf_op jit(solution)/shard_map/all_gather | solution.py:155
Sparse Core Ops, SparseCore 0:
  67.5 64.9 reduce-scatter.1
  139.4 39.0 all-gather.1

commit v2 on v1

--- a/solution.py
+++ b/solution.py
@@ -9,6 +9,7 @@
 from jax.sharding import PartitionSpec as P
 
 LANES = 128
+MESH = pl.DeviceIdType.MESH
 
 
 def dft_tables(length):
@@ -73,28 +74,154 @@
     return total
 
 
-def elements_kernel(length, owners, tile, codes_ref, valence_ref, conduction_ref, first_ref,
-                    second_ref, xtable_ref, out_ref, planes, left):
+def gather_kernel(length, bands_axis, owners, tile, codes_ref, factor_ref, valence_ref, conduction_ref,
+                  first_ref, second_ref, xtable_ref, rows_ref, owned_ref,
+                  planes, left, codes_all, partial, arrived, row_parts, owned_parts,
+                  code_send, code_recv, part_send, part_recv, row_send, row_recv, own_send, own_recv):
     pairs = valence_ref.shape[0] * conduction_ref.shape[0]
     slab = valence_ref.shape[1]
     rows = 2 * slab * pairs
-    own = codes_ref.shape[1] // owners
+    own = codes_ref.shape[1]
+    half = own // 2
     yslab = length // owners
+    ratio = owned_parts.shape[0]
+    band = lax.axis_index("band")
+    me = lax.axis_index("fft")
+
+    def around(shift):
+        return lax.rem(me + shift, owners)
+
+    def across(shift):
+        return lax.rem(band + shift, bands_axis)
+
+    barrier = pltpu.get_barrier_semaphore()
+
+    def greet_fft(shift, carry):
+        pl.semaphore_signal(barrier, inc=1, device_id=(band, around(shift)), device_id_type=MESH)
+        return carry
+
+    def greet_band(shift, carry):
+        pl.semaphore_signal(barrier, inc=1, device_id=(across(shift), me), device_id_type=MESH)
+        return carry
+
+    lax.fori_loop(1, owners, greet_fft, 0)
+    lax.fori_loop(1, bands_axis, greet_band, 0)
+    pl.semaphore_wait(barrier, owners + bands_axis - 2)
+
+    def code_copy(shift):
+        return pltpu.make_async_remote_copy(
+            src_ref=codes_ref, dst_ref=codes_all.at[shift],
+            send_sem=code_send.at[shift], recv_sem=code_recv.at[shift],
+            device_id=(band, around(shift)), device_id_type=MESH,
+        )
+
+    def part_copy(shift):
+        return pltpu.make_async_remote_copy(
+            src_ref=partial.at[shift], dst_ref=arrived.at[shift],
+            send_sem=part_send.at[shift], recv_sem=part_recv.at[shift],
+            device_id=(band, around(owners - shift)), device_id_type=MESH,
+        )
+
+    def row_copy(shift):
+        return pltpu.make_async_remote_copy(
+            src_ref=row_parts.at[band], dst_ref=row_parts.at[band],
+            send_sem=row_send.at[shift], recv_sem=row_recv.at[shift],
+            device_id=(across(shift), me), device_id_type=MESH,
+        )
+
+    def row_wait(shift):
+        source = across(bands_axis - shift)
+        return pltpu.make_async_remote_copy(
+            src_ref=row_parts.at[band], dst_ref=row_parts.at[source],
+            send_sem=row_send.at[shift], recv_sem=row_recv.at[shift],
+            device_id=(across(shift), me), device_id_type=MESH,
+        )
+
+    def owned_copy(shift, slot):
+        return pltpu.make_async_remote_copy(
+            src_ref=row_parts, dst_ref=owned_parts.at[slot],
+            send_sem=own_send.at[shift], recv_sem=own_recv.at[slot],
+            device_id=(band, around(shift)), device_id_type=MESH,
+        )
+
+    def each(first, last, act):
+        def step(i, carry):
+            act(i)
+            return carry
+
+        lax.fori_loop(first, last, step, 0)
+
+    each(1, owners, lambda s: code_copy(s).start())
+    codes_all[0] = codes_ref[...]
     transform(valence_ref, conduction_ref, first_ref, second_ref, planes, length)
 
-    def one_owner(o, carry):
+    def one_owner(step):
+        shift = lax.rem(step, owners)
+        o = lax.rem(me + owners - shift, owners)
+
+        @pl.when(shift > 0)
+        def _():
+            code_copy(shift).wait_recv()
+
         for k in range(yslab):
             part = planes[pl.ds(pl.multiple_of((o * yslab + k) * rows, rows), rows), :]
             left[:, k * LANES : (k + 1) * LANES] = part.astype(jnp.bfloat16)
 
-        def one_tile(t, carry):
-            at = pl.ds(pl.multiple_of(o * own + t * tile, tile), tile)
-            out_ref[:, at] = sample_tile(codes_ref[:, at], left, xtable_ref, pairs, slab)
-            return carry
-
-        return lax.fori_loop(0, own // tile, one_tile, carry)
-
-    lax.fori_loop(0, owners, one_owner, 0)
+        for t in range(0, own, tile):
+            codes = codes_all[shift, :, t : t + tile]
+            partial[shift, :, t : t + tile] = sample_tile(codes, left, xtable_ref, pairs, slab)
+
+        @pl.when(shift > 0)
+        def _():
+            part_copy(shift).start()
+
+    each(1, owners + 1, one_owner)
+    each(1, owners, lambda s: code_copy(s).wait_send())
+
+    each(1, owners, lambda s: part_copy(s).wait_recv())
+    total = partial[0]
+    for s in range(1, owners):
+        total += arrived[s]
+    scaled = factor_ref[:, :1] * total
+    row_parts[band] = jnp.concatenate([scaled[:, :half], scaled[:, half:]], axis=0).astype(jnp.bfloat16)
+    each(1, bands_axis, lambda s: row_copy(s).start())
+    each(1, bands_axis, lambda s: row_wait(s).wait_recv())
+
+    mine = me // ratio == band
+    slot = lax.rem(me, ratio)
+
+    @pl.when(mine)
+    def _():
+        each(1, owners, lambda s: owned_copy(s, slot).start())
+        owned_parts[slot] = row_parts[...]
+
+    def join(parts):
+        parts = parts.astype(jnp.float32)
+        halves = [parts[:, h * pairs : (h + 1) * pairs].reshape(bands_axis * pairs, half) for h in range(2)]
+        return jnp.concatenate(halves, axis=1)
+
+    rows_ref[...] = join(row_parts[...]).astype(jnp.bfloat16)
+    for j in range(ratio):
+
+        @pl.when(band * ratio + j != me)
+        def _():
+            owned_copy(1, j).wait_recv()
+
+        owned_ref[:, j * own : (j + 1) * own] = (-join(owned_parts[j])).astype(jnp.bfloat16)
+
+    each(1, owners, lambda s: part_copy(s).wait_send())
+    each(1, bands_axis, lambda s: row_copy(s).wait_send())
+
+    @pl.when(mine)
+    def _():
+        each(1, owners, lambda s: owned_copy(s, slot).wait_send())
+
+
+def product_kernel(rows_ref, owned_ref, out_ref):
+    contract = (((0,), (0,)), ((), ()))
+    out_ref[...] = lax.dot_general(
+        rows_ref[...], owned_ref[...], contract, preferred_element_type=jnp.float32
+    )
 
 
 def on_device(valence_waves, conduction_waves, valence_energy, conduction_energy, sphere_slots):
@@ -107,6 +234,7 @@
     pairs_all = groups * pairs
     own = sphere_slots.shape[0]
     yslab = length // owners
+    ratio = owners // groups
     me = lax.axis_index("fft")
 
     table_cos, table_sin = dft_tables(length)
@@ -131,32 +259,55 @@
     ky = (sphere_slots // width) % yslab
     comp = sphere_slots % width
     imag = (comp >= length).astype(jnp.int32)
-    codes = kx + ((ky * LANES + comp - imag * length) << 8) + (imag << 20)
-    codes = lax.all_gather(codes, "fft", axis=0, tiled=True)[None]
-
-    partial = pl.pallas_call(
-        functools.partial(elements_kernel, length, owners, min(512, own)),
-        out_shape=jax.ShapeDtypeStruct((pairs, owners * own), jnp.float32),
-        in_specs=[pl.BlockSpec(memory_space=pltpu.VMEM)] * 6,
-        out_specs=pl.BlockSpec(memory_space=pltpu.VMEM),
+    codes = (kx + ((ky * LANES + comp - imag * length) << 8) + (imag << 20))[None]
+    spacing = conduction_energy[None, :] - valence_energy[:, None]
+    factor = jnp.sqrt(4.0 / (spacing * pairs_all)).reshape(pairs)
+    factor = jnp.broadcast_to(factor[:, None], (pairs, LANES))
+
+    rows, owned = pl.pallas_call(
+        functools.partial(gather_kernel, length, groups, owners, min(512, own)),
+        out_shape=(
+            jax.ShapeDtypeStruct((pairs_all, own), jnp.bfloat16),
+            jax.ShapeDtypeStruct((pairs_all, ratio * own), jnp.bfloat16),
+        ),
+        in_specs=[pl.BlockSpec(memory_space=pltpu.VMEM)] * 7,
+        out_specs=(pl.BlockSpec(memory_space=pltpu.VMEM), pl.BlockSpec(memory_space=pltpu.VMEM)),
         scratch_shapes=[
             pltpu.VMEM((2 * length * slab * pairs, LANES), jnp.float32),
             pltpu.VMEM((2 * slab * pairs, yslab * LANES), jnp.bfloat16),
+            pltpu.VMEM((owners, 1, own), jnp.int32),
+            pltpu.VMEM((owners, pairs, own), jnp.float32),
+            pltpu.VMEM((owners, pairs, own), jnp.float32),
+            pltpu.VMEM((groups, 2 * pairs, own // 2), jnp.bfloat16),
+            pltpu.VMEM((ratio, groups, 2 * pairs, own // 2), jnp.bfloat16),
+            pltpu.SemaphoreType.DMA((owners,)),
+            pltpu.SemaphoreType.DMA((owners,)),
+            pltpu.SemaphoreType.DMA((owners,)),
+            pltpu.SemaphoreType.DMA((owners,)),
+            pltpu.SemaphoreType.DMA((groups,)),
+            pltpu.SemaphoreType.DMA((groups,)),
+            pltpu.SemaphoreType.DMA((owners,)),
+            pltpu.SemaphoreType.DMA((ratio,)),
         ],
+        compiler_params=pltpu.CompilerParams(
+            collective_id=0, has_side_effects=True, vmem_limit_bytes=48 * 2**20
+        ),
+        name="gather",
+    )(codes, factor, valence_waves, conduction_waves, first_table, second_table, xtable)
+
+    tile = min(256, own)
+    return pl.pallas_call(
+        product_kernel,
+        grid=(own // tile,),
+        out_shape=jax.ShapeDtypeStruct((own, ratio * own), jnp.float32),
+        in_specs=[
+            pl.BlockSpec((pairs_all, tile), lambda i: (0, i)),
+            pl.BlockSpec((pairs_all, ratio * own), lambda i: (0, 0)),
+        ],
+        out_specs=pl.BlockSpec((tile, ratio * own), lambda i: (i, 0)),
         compiler_params=pltpu.CompilerParams(vmem_limit_bytes=48 * 2**20),
-        name="elements",
-    )(codes, valence_waves, conduction_waves, first_table, second_table, xtable)
-    elements = lax.psum_scatter(partial, "fft", scatter_dimension=1, tiled=True)
-    spacing = conduction_energy[None, :] - valence_energy[:, None]
-    factor = jnp.sqrt(4.0 / (spacing * pairs_all)).reshape(pairs)
-    scaled = (factor[:, None] * elements).astype(jnp.bfloat16)
-
-    rows = lax.all_gather(scaled, "band", axis=0, tiled=True)
-    whole = lax.all_gather(rows, "fft", axis=1, tiled=True)
-    share = owners * own // groups
-    owned = lax.dynamic_slice_in_dim(whole, lax.axis_index("band") * share, share, axis=1)
-    contract = (((0,), (0,)), ((), ()))
-    return -lax.dot_general(rows, owned, contract, preferred_element_type=jnp.float32)
+        name="product",
+    )(rows, owned)
 
 
 def solution(mesh):

time: 206 us -> 65.8 us (0.32)
  the two profiles are of different devices: /device:TPU:24 before, /device:TPU:14 now
where the time goes in v2:
time: 65.8 us; the launch traced here: 65.6 us
  Pallas kernels  60.7 us (92%)
  local copies, waits for them, and re-layouts  2.73 us (4%)
  other arithmetic  2.06 us (3%)
    pallas_call x1, Pallas kernels, on_device(): pl.pallas_call(functools.partial(gather_kernel, length, groups, owners, m...  48.3 us
    pallas_call x1, Pallas kernels, on_device(): pl.pallas_call(product_kernel, grid=(own // tile,), out_shape=jax.ShapeDt...  12.4 us
    unnamed x4, local copies, waits for them, and re-layouts  2.33 us

profile of v2, /device:TPU:14, one launch (start us, length us, event | category | flops | bytes accessed | tf_op | source)
XLA Modules:
  0.0 65.6 jit_solution(14756782262903965078)
XLA Ops:
  0.0 0.7 %divide_sqrt_fusion = f32[2,4]{1,0:T(2,128)S(1)} fusion(f32[4]{0:T(128)} %param.8, f32[2]{0:T(128)} %param.7), kind=kLoop, calls=%fused_computation.39 | loop fusion | flops 24 | bytes 56 | tf_op jit(solution)/shard_map/sqrt | solution.py:264
  0.7 0.1 sqrt.11
  0.8 0.1 broadcast_in_dim.5.factor_ref
  0.9 0.7 %fusion.12 = s32[2048]{0:T(1024)S(1)} fusion(s32[2048]{0:T(1024)} %param.9), kind=kLoop, calls=%fused_computation.27 | loop fusion | flops 69632 | bytes 16384 | tf_op jit(solution)/shard_map/add | solution.py:262
  1.6 0.2 fusion.10
  1.9 0.2 multiply_convert_fusion
  2.2 0.1 maximum_bitcast_fusion
  2.3 0.1 copy.6
  2.4 0.1 reshape.27.second_ref
  2.5 0.0 copy-start
  2.5 1.3 %copy-done = bf16[4,12,96,96]{3,2,1,0:T(8,128)(2,1)S(1)} copy-done((bf16[4,12,96,96]{3,2,1,0:T(8,128)(2,1)S(1)}, bf16[4,12,96,96]{3,2,1,0:T(8,128)(2,1)}, u32[]{:S(2)}) %copy-start) | copy-done | bytes 884760
  3.8 0.0 copy-start.1
  3.8 1.1 %copy-done.1 = bf16[2,12,96,96]{3,2,1,0:T(8,128)(2,1)S(1)} copy-done((bf16[2,12,96,96]{3,2,1,0:T(8,128)(2,1)S(1)}, bf16[2,12,96,96]{3,2,1,0:T(8,128)(2,1)}, u32[]{:S(2)}) %copy-start.1) | copy-done | bytes 442392
  4.9 48.3 %gather.1 = (bf16[32,2048]{1,0:T(8,128)(2,1)S(1)}, bf16[32,4096]{1,0:T(8,128)(2,1)S(1)}) custom-call(s32[1,2048]{1,0:T(1,128)S(1)} %bitcast.5, f32[8,128]{1,0:T(8,128)S(1)} %broadcast_in_dim.5.factor_ref, bf16[2,12,96,96]{3,2,1,0:T(8,128)(2,1)S(1)} %copy-done.1, bf16[4,12,96,96]{3,2,1,0:T(8,128)(2,1)S(1)} %copy-done, bf16[96,256]{1,0:T(8,128)(2,1)S(1)} %fusion.4.first_ref, ...), custom_call_target="tpu_custom_call" | custom-call | tf_op jit(solution)/shard_map/gather/pallas_call | solution.py:267
  53.2 12.4 %product.1 = f32[2048,4096]{1,0:T(8,128)} custom-call(bf16[32,2048]{1,0:T(8,128)(2,1)S(1)} %get-tuple-element.7.rows_ref, bf16[32,4096]{1,0:T(8,128)(2,1)S(1)} %get-tuple-element.8.owned_ref), custom_call_target="tpu_custom_call" | custom-call | tf_op jit(solution)/shard_map/product/pallas_call | solution.py:299
  (5 shorter events, 0.1 us)
Async XLA Ops:
  2.5 1.3 %copy-start = (bf16[4,12,96,96]{3,2,1,0:T(8,128)(2,1)S(1)}, bf16[4,12,96,96]{3,2,1,0:T(8,128)(2,1)}, u32[]{:S(2)}) copy-start(bf16[4,12,96,96]{3,2,1,0:T(8,128)(2,1)} %conduction_ref.1) | copy-start | bytes 2654212
  3.8 1.1 %copy-start.1 = (bf16[2,12,96,96]{3,2,1,0:T(8,128)(2,1)S(1)}, bf16[2,12,96,96]{3,2,1,0:T(8,128)(2,1)}, u32[]{:S(2)}) copy-start(bf16[2,12,96,96]{3,2,1,0:T(8,128)(2,1)} %valence_ref.1) | copy-start | bytes 1327108

commit v3 on v2

--- a/solution.py
+++ b/solution.py
@@ -74,10 +74,12 @@
     return total
 
 
-def gather_kernel(length, bands_axis, owners, tile, codes_ref, factor_ref, valence_ref, conduction_ref,
-                  first_ref, second_ref, xtable_ref, rows_ref, owned_ref,
-                  planes, left, codes_all, partial, arrived, row_parts, owned_parts,
-                  code_send, code_recv, part_send, part_recv, row_send, row_recv, own_send, own_recv):
+def gather_kernel(length, bands_axis, owners, tile, codes_ref, valence_energy, conduction_energy,
+                  valence_hbm, conduction_hbm, first_ref, second_ref, xtable_ref, rows_ref, owned_ref,
+                  valence_ref, conduction_ref, planes, left, codes_all, work, partial, arrived,
+                  row_parts, owned_parts, load_sem,
+                  code_send, code_recv, part_send, part_recv, row_send, row_recv, own_send, own_recv,
+                  side_send, side_recv):
     pairs = valence_ref.shape[0] * conduction_ref.shape[0]
     slab = valence_ref.shape[1]
     rows = 2 * slab * pairs
@@ -87,6 +89,14 @@
     ratio = owned_parts.shape[0]
     band = lax.axis_index("band")
     me = lax.axis_index("fft")
+    root = me // ratio
+    slot = lax.rem(me, ratio)
+    loads = [
+        pltpu.make_async_copy(valence_hbm, valence_ref, load_sem.at[0]),
+        pltpu.make_async_copy(conduction_hbm, conduction_ref, load_sem.at[1]),
+    ]
+    for load in loads:
+        load.start()
 
     def around(shift):
         return lax.rem(me + shift, owners)
@@ -137,11 +147,20 @@
             device_id=(across(shift), me), device_id_type=MESH,
         )
 
-    def owned_copy(shift, slot):
-        return pltpu.make_async_remote_copy(
-            src_ref=row_parts, dst_ref=owned_parts.at[slot],
-            send_sem=own_send.at[shift], recv_sem=own_recv.at[slot],
-            device_id=(band, around(shift)), device_id_type=MESH,
+    def owned_copy(hop, shift):
+        chunk = across(bands_axis - shift)
+        return pltpu.make_async_remote_copy(
+            src_ref=owned_parts.at[slot, chunk], dst_ref=owned_parts.at[slot, chunk],
+            send_sem=own_send.at[hop, shift], recv_sem=own_recv.at[shift],
+            device_id=(band, across(hop) * ratio + slot), device_id_type=MESH,
+        )
+
+    def side_copy(hop, shift, source):
+        chunk = across(bands_axis - shift)
+        return pltpu.make_async_remote_copy(
+            src_ref=owned_parts.at[source, chunk], dst_ref=owned_parts.at[source, chunk],
+            send_sem=side_send.at[hop, shift], recv_sem=side_recv.at[hop, shift],
+            device_id=(band, root * ratio + lax.rem(slot + hop, ratio)), device_id_type=MESH,
         )
 
     def each(first, last, act):
@@ -153,7 +172,12 @@
 
     each(1, owners, lambda s: code_copy(s).start())
     codes_all[0] = codes_ref[...]
+    for load in loads:
+        load.wait()
     transform(valence_ref, conduction_ref, first_ref, second_ref, planes, length)
+
+    def folded(array):
+        return jnp.concatenate([array[:, :half], array[:, half:]], axis=0)
 
     def one_owner(step):
         shift = lax.rem(step, owners)
@@ -169,31 +193,52 @@
 
         for t in range(0, own, tile):
             codes = codes_all[shift, :, t : t + tile]
-            partial[shift, :, t : t + tile] = sample_tile(codes, left, xtable_ref, pairs, slab)
+            work[:, t : t + tile] = sample_tile(codes, left, xtable_ref, pairs, slab)
 
         @pl.when(shift > 0)
         def _():
+            partial[shift] = folded(work).astype(jnp.bfloat16)
             part_copy(shift).start()
 
     each(1, owners + 1, one_owner)
     each(1, owners, lambda s: code_copy(s).wait_send())
 
-    each(1, owners, lambda s: part_copy(s).wait_recv())
-    total = partial[0]
+    line = lax.broadcasted_iota(jnp.int32, (2 * pairs, LANES), 0)
+    spacing = jnp.ones((2 * pairs, LANES), jnp.float32)
+    bands = conduction_ref.shape[0]
+    for p in range(2 * pairs):
+        v, c = p % pairs // bands, p % bands
+        spacing = jnp.where(line == p, conduction_energy[c] - valence_energy[v], spacing)
+    factor = jnp.sqrt(4.0 / (spacing * (bands_axis * pairs)))
+
+    total = folded(work)
     for s in range(1, owners):
-        total += arrived[s]
-    scaled = factor_ref[:, :1] * total
-    row_parts[band] = jnp.concatenate([scaled[:, :half], scaled[:, half:]], axis=0).astype(jnp.bfloat16)
+        part_copy(s).wait_recv()
+        total += arrived[s].astype(jnp.float32)
+    row_parts[band] = (factor[:, :1] * total).astype(jnp.bfloat16)
     each(1, bands_axis, lambda s: row_copy(s).start())
-    each(1, bands_axis, lambda s: row_wait(s).wait_recv())
-
-    mine = me // ratio == band
-    slot = lax.rem(me, ratio)
-
-    @pl.when(mine)
-    def _():
-        each(1, owners, lambda s: owned_copy(s, slot).start())
-        owned_parts[slot] = row_parts[...]
+    mine = root == band
+
+    def one_chunk(shift):
+        chunk = across(bands_axis - shift)
+
+        @pl.when(shift > 0)
+        def _():
+            row_wait(shift).wait_recv()
+
+        @pl.when(mine)
+        def _():
+            owned_parts[slot, chunk] = row_parts[chunk]
+            each(1, bands_axis, lambda hop: owned_copy(hop, shift).start())
+
+        @pl.when(jnp.logical_not(mine))
+        def _():
+            owned_copy(0, shift).wait_recv()
+
+        for hop in range(1, ratio):
+            side_copy(hop, shift, slot).start()
+
+    each(0, bands_axis, one_chunk)
 
     def join(parts):
         parts = parts.astype(jnp.float32)
@@ -201,12 +246,10 @@
         return jnp.concatenate(halves, axis=1)
 
     rows_ref[...] = join(row_parts[...]).astype(jnp.bfloat16)
+    for hop in range(1, ratio):
+        source = lax.rem(slot + ratio - hop, ratio)
+        each(0, bands_axis, lambda s: side_copy(hop, s, source).wait_recv())
     for j in range(ratio):
-
-        @pl.when(band * ratio + j != me)
-        def _():
-            owned_copy(1, j).wait_recv()
-
         owned_ref[:, j * own : (j + 1) * own] = (-join(owned_parts[j])).astype(jnp.bfloat16)
 
     each(1, owners, lambda s: part_copy(s).wait_send())
@@ -214,7 +257,10 @@
 
     @pl.when(mine)
     def _():
-        each(1, owners, lambda s: owned_copy(s, slot).wait_send())
+        each(0, bands_axis, lambda s: each(1, bands_axis, lambda hop: owned_copy(hop, s).wait_send()))
+
+    for hop in range(1, ratio):
+        each(0, bands_axis, lambda s: side_copy(hop, s, slot).wait_send())
 
 
 def product_kernel(rows_ref, owned_ref, out_ref):
@@ -260,42 +306,47 @@
     comp = sphere_slots % width
     imag = (comp >= length).astype(jnp.int32)
     codes = (kx + ((ky * LANES + comp - imag * length) << 8) + (imag << 20))[None]
-    spacing = conduction_energy[None, :] - valence_energy[:, None]
-    factor = jnp.sqrt(4.0 / (spacing * pairs_all)).reshape(pairs)
-    factor = jnp.broadcast_to(factor[:, None], (pairs, LANES))
-
     rows, owned = pl.pallas_call(
         functools.partial(gather_kernel, length, groups, owners, min(512, own)),
         out_shape=(
             jax.ShapeDtypeStruct((pairs_all, own), jnp.bfloat16),
             jax.ShapeDtypeStruct((pairs_all, ratio * own), jnp.bfloat16),
         ),
-        in_specs=[pl.BlockSpec(memory_space=pltpu.VMEM)] * 7,
+        in_specs=[pl.BlockSpec(memory_space=pltpu.VMEM)]
+        + [pl.BlockSpec(memory_space=pltpu.SMEM)] * 2
+        + [pl.BlockSpec(memory_space=pl.ANY)] * 2
+        + [pl.BlockSpec(memory_space=pltpu.VMEM)] * 3,
         out_specs=(pl.BlockSpec(memory_space=pltpu.VMEM), pl.BlockSpec(memory_space=pltpu.VMEM)),
         scratch_shapes=[
+            pltpu.VMEM(valence_waves.shape, jnp.bfloat16),
+            pltpu.VMEM(conduction_waves.shape, jnp.bfloat16),
             pltpu.VMEM((2 * length * slab * pairs, LANES), jnp.float32),
             pltpu.VMEM((2 * slab * pairs, yslab * LANES), jnp.bfloat16),
             pltpu.VMEM((owners, 1, own), jnp.int32),
-            pltpu.VMEM((owners, pairs, own), jnp.float32),
-            pltpu.VMEM((owners, pairs, own), jnp.float32),
+            pltpu.VMEM((pairs, own), jnp.float32),
+            pltpu.VMEM((owners, 2 * pairs, own // 2), jnp.bfloat16),
+            pltpu.VMEM((owners, 2 * pairs, own // 2), jnp.bfloat16),
             pltpu.VMEM((groups, 2 * pairs, own // 2), jnp.bfloat16),
             pltpu.VMEM((ratio, groups, 2 * pairs, own // 2), jnp.bfloat16),
+            pltpu.SemaphoreType.DMA((2,)),
             pltpu.SemaphoreType.DMA((owners,)),
             pltpu.SemaphoreType.DMA((owners,)),
             pltpu.SemaphoreType.DMA((owners,)),
             pltpu.SemaphoreType.DMA((owners,)),
             pltpu.SemaphoreType.DMA((groups,)),
             pltpu.SemaphoreType.DMA((groups,)),
-            pltpu.SemaphoreType.DMA((owners,)),
-            pltpu.SemaphoreType.DMA((ratio,)),
+            pltpu.SemaphoreType.DMA((groups, groups)),
+            pltpu.SemaphoreType.DMA((groups,)),
+            pltpu.SemaphoreType.DMA((ratio, groups)),
+            pltpu.SemaphoreType.DMA((ratio, groups)),
         ],
         compiler_params=pltpu.CompilerParams(
             collective_id=0, has_side_effects=True, vmem_limit_bytes=48 * 2**20
         ),
         name="gather",
-    )(codes, factor, valence_waves, conduction_waves, first_table, second_table, xtable)
-
-    tile = min(256, own)
+    )(codes, valence_energy, conduction_energy, valence_waves, conduction_waves, first_table, second_table, xtable)
+
+    tile = min(128, own)
     return pl.pallas_call(
         product_kernel,
         grid=(own // tile,),

time: 65.8 us -> 63.5 us (0.965)
  the two profiles are of different devices: /device:TPU:14 before, /device:TPU:24 now
where the time goes in v3:
time: 63.5 us; the launch traced here: 63.2 us
  Pallas kernels  58 us (91%)
  local copies, waits for them, and re-layouts  3.88 us (6%)
  other arithmetic  1.31 us (2%)
    pallas_call x1, Pallas kernels, on_device(): pl.pallas_call(functools.partial(gather_kernel, length, groups, owners, m...  43 us
    pallas_call x1, Pallas kernels, on_device(): pl.pallas_call(product_kernel, grid=(own // tile,), out_shape=jax.ShapeDt...  14.9 us
    unnamed x8, local copies, waits for them, and re-layouts  3.64 us

profile of v3, /device:TPU:24, one launch (start us, length us, event | category | flops | bytes accessed | tf_op | source)
XLA Modules:
  0.0 63.2 jit_solution(497639057330026372)
XLA Ops:
  0.0 0.7 %fusion.12 = s32[2048]{0:T(1024)S(1)} fusion(s32[2048]{0:T(1024)} %param.9), kind=kLoop, calls=%fused_computation.27 | loop fusion | flops 69632 | bytes 16384 | tf_op jit(solution)/shard_map/add | solution.py:308
  0.7 0.2 fusion.10
  0.9 0.2 multiply_convert_fusion
  1.3 0.1 maximum_bitcast_fusion
  1.4 0.1 copy.6
  1.5 0.1 reshape.3.second_ref
  1.6 0.0 copy-start
  1.6 1.3 %copy-done = bf16[4,12,96,96]{3,2,1,0:T(8,128)(2,1)S(1)} copy-done((bf16[4,12,96,96]{3,2,1,0:T(8,128)(2,1)S(1)}, bf16[4,12,96,96]{3,2,1,0:T(8,128)(2,1)}, u32[]{:S(2)}) %copy-start) | copy-done | bytes 884760
  2.9 0.0 copy-start.1
  2.9 1.1 %copy-done.1 = bf16[2,12,96,96]{3,2,1,0:T(8,128)(2,1)S(1)} copy-done((bf16[2,12,96,96]{3,2,1,0:T(8,128)(2,1)S(1)}, bf16[2,12,96,96]{3,2,1,0:T(8,128)(2,1)}, u32[]{:S(2)}) %copy-start.1) | copy-done | bytes 442392
  4.0 0.0 copy-start.2
  4.0 0.7 %copy-done.2 = f32[2]{0:T(128)S(1)} copy-done((f32[2]{0:T(128)S(1)}, f32[2]{0:T(128)}, u32[]{:S(2)}) %copy-start.2) | copy-done | bytes 32
  4.6 0.0 copy-start.3
  4.6 0.7 %copy-done.3 = f32[4]{0:T(128)S(1)} copy-done((f32[4]{0:T(128)S(1)}, f32[4]{0:T(128)}, u32[]{:S(2)}) %copy-start.3) | copy-done | bytes 40
  5.3 43.0 %gather.1 = (bf16[32,2048]{1,0:T(8,128)(2,1)S(1)}, bf16[32,4096]{1,0:T(8,128)(2,1)S(1)}) custom-call(s32[1,2048]{1,0:T(1,128)S(1)} %bitcast.5, f32[2]{0:T(128)S(1)} %copy-done.2, f32[4]{0:T(128)S(1)} %copy-done.3, bf16[2,12,96,96]{3,2,1,0:T(8,128)(2,1)S(1)} %copy-done.1, bf16[4,12,96,96]{3,2,1,0:T(8,128)(2,1)S(1)} %copy-done, ...), custom_call_target="tpu_custom_call" | custom-call | tf_op jit(solution)/shard_map/gather/pallas_call | solution.py:309
  48.3 14.9 %product.1 = f32[2048,4096]{1,0:T(8,128)} custom-call(bf16[32,2048]{1,0:T(8,128)(2,1)S(1)} %get-tuple-element.7.rows_ref, bf16[32,4096]{1,0:T(8,128)(2,1)S(1)} %get-tuple-element.8.owned_ref), custom_call_target="tpu_custom_call" | custom-call | tf_op jit(solution)/shard_map/product/pallas_call | solution.py:350
  (5 shorter events, 0.1 us)
Async XLA Ops:
  1.6 1.3 %copy-start = (bf16[4,12,96,96]{3,2,1,0:T(8,128)(2,1)S(1)}, bf16[4,12,96,96]{3,2,1,0:T(8,128)(2,1)}, u32[]{:S(2)}) copy-start(bf16[4,12,96,96]{3,2,1,0:T(8,128)(2,1)} %conduction_hbm.1) | copy-start | bytes 2654212
  2.9 1.1 %copy-start.1 = (bf16[2,12,96,96]{3,2,1,0:T(8,128)(2,1)S(1)}, bf16[2,12,96,96]{3,2,1,0:T(8,128)(2,1)}, u32[]{:S(2)}) copy-start(bf16[2,12,96,96]{3,2,1,0:T(8,128)(2,1)} %valence_hbm.1) | copy-start | bytes 1327108
  4.0 0.7 %copy-start.2 = (f32[2]{0:T(128)S(1)}, f32[2]{0:T(128)}, u32[]{:S(2)}) copy-start(f32[2]{0:T(128)} %valence_energy.1) | copy-start | bytes 28
  4.6 0.7 %copy-start.3 = (f32[4]{0:T(128)S(1)}, f32[4]{0:T(128)}, u32[]{:S(2)}) copy-start(f32[4]{0:T(128)} %conduction_energy.1) | copy-start | bytes 52

commit v4 on v3

--- a/solution.py
+++ b/solution.py
@@ -54,10 +54,15 @@
     tile = codes.shape[1]
     depth = left.shape[1]
     kx = codes & 255
-    column = (codes >> 8) & 4095
+    q = (codes >> 8) & (LANES - 1)
+    ky = (codes >> 15) & 31
     imag = (codes >> 20) > 0
-    hot = lax.broadcasted_iota(jnp.int32, (depth, tile), 0) == column
-    hot = jnp.where(hot, 1.0, 0.0).astype(jnp.bfloat16)
+    hot_q = lax.broadcasted_iota(jnp.int32, (LANES, tile), 0) == q
+    hot_q = jnp.where(hot_q, 1.0, 0.0).astype(jnp.bfloat16)
+    blocks = []
+    for k in range(depth // LANES):
+        blocks.append(hot_q * jnp.where(ky == k, 1.0, 0.0).astype(jnp.bfloat16))
+    hot = jnp.concatenate(blocks, axis=0)
     picked = jnp.dot(left[...], hot, preferred_element_type=jnp.float32)
     hot_x = lax.broadcasted_iota(jnp.int32, (LANES, tile), 0) == kx
     hot_x = jnp.where(hot_x, 1.0, 0.0).astype(jnp.bfloat16)
@@ -341,12 +346,12 @@
             pltpu.SemaphoreType.DMA((ratio, groups)),
         ],
         compiler_params=pltpu.CompilerParams(
-            collective_id=0, has_side_effects=True, vmem_limit_bytes=48 * 2**20
+            collective_id=0, has_side_effects=True, vmem_limit_bytes=60 * 2**20
         ),
         name="gather",
     )(codes, valence_energy, conduction_energy, valence_waves, conduction_waves, first_table, second_table, xtable)
 
-    tile = min(128, own)
+    tile = min(256, own)
     return pl.pallas_call(
         product_kernel,
         grid=(own // tile,),

time: 63.5 us -> 60.8 us (0.957)
  Pallas kernels: 58 us -> 54.7 us
  other arithmetic: 1.31 us -> 3.1 us
  local copies, waits for them, and re-layouts: 3.88 us -> 2.73 us
    pallas_call x1, Pallas kernels: 14.9 us -> 12.3 us  [on_device(): pl.pallas_call(product_kernel, grid=(own // tile,), out_shape=jax.ShapeDt...]
    unnamed x8 -> x4, local copies, waits for them, and re-layouts: 3.64 us -> 1.85 us
    pallas_call x1, Pallas kernels: 43 us -> 42.3 us  [on_device(): pl.pallas_call(functools.partial(gather_kernel, length, groups, owners, m...]
    reshape x1, local copies, waits for them, and re-layouts: 0.1 us -> 0.74 us  [on_device(): second_table = jnp.stack([jnp.concatenate([table_cos, table_sin], axis=1)...]
where the time goes in v4:
time: 60.8 us; the launch traced here: 60.5 us
  Pallas kernels  54.7 us (90%)
  other arithmetic  3.1 us (5%)
  local copies, waits for them, and re-layouts  2.73 us (4%)
    pallas_call x1, Pallas kernels, on_device(): pl.pallas_call(functools.partial(gather_kernel, length, groups, owners, m...  42.3 us
    pallas_call x1, Pallas kernels, on_device(): pl.pallas_call(product_kernel, grid=(own // tile,), out_shape=jax.ShapeDt...  12.3 us
    unnamed x4, local copies, waits for them, and re-layouts  1.85 us
    add x1, other arithmetic, on_device(): codes = (kx + (ky * LANES + comp - imag * length << 8) + (imag << 20))[None]  1.32 us

profile of v4, /device:TPU:24, one launch (start us, length us, event | category | flops | bytes accessed | tf_op | source)
XLA Modules:
  0.0 60.5 jit_solution(18329305582694662676)
XLA Ops:
  0.0 1.3 %fusion.12 = s32[2048]{0:T(1024)} fusion(s32[2048]{0:T(1024)} %param.9), kind=kLoop, calls=%fused_computation.27 | loop fusion | flops 69632 | bytes 16384 | tf_op jit(solution)/shard_map/add | solution.py:313
  1.3 0.2 fusion.10
  1.5 0.2 multiply_convert_fusion
  1.8 0.6 fusion.18.xtable_ref
  2.4 0.6 %fusion.4.first_ref = bf16[96,256]{1,0:T(8,128)(2,1)} fusion(bf16[96,96]{1,0:T(8,128)(2,1)S(1)} %fusion.10, bf16[96,96]{1,0:T(8,128)(2,1)S(1)} %get-tuple-element.12), kind=kLoop, calls=%fused_computation.8 | loop fusion | flops 196608 | bytes 86016 | tf_op jit(solution)/shard_map/concatenate | solution.py:293
  3.0 0.1 maximum_bitcast_fusion
  3.2 0.1 copy.6
  3.3 0.7 %reshape.3.second_ref = bf16[192,192]{1,0:T(8,128)(2,1)} reshape(bf16[96,2,192]{2,1,0:T(2,128)(2,1)S(1)} %copy.6) | data formatting | bytes 147456 | tf_op jit(solution)/shard_map/reshape | solution.py:300
  4.0 42.3 %gather.1 = (bf16[32,2048]{1,0:T(8,128)(2,1)}, bf16[32,4096]{1,0:T(8,128)(2,1)}) custom-call(s32[1,2048]{1,0:T(1,128)} %bitcast.5, f32[2]{0:T(128)} %valence_energy.1, f32[4]{0:T(128)} %conduction_energy.1, bf16[2,12,96,96]{3,2,1,0:T(8,128)(2,1)} %valence_hbm.1, bf16[4,12,96,96]{3,2,1,0:T(8,128)(2,1)} %conduction_hbm.1, bf16[96,256]{1,0:T(8,128)(2,1)} %fusion.4.first_ref, ...), custom_call_target="tpu_custom_call" | custom-call | tf_op jit(solution)/shard_map/gather/pallas_call | solution.py:314
  46.3 0.0 copy-start
  46.4 0.9 %copy-done = bf16[32,4096]{1,0:T(8,128)(2,1)S(1)} copy-done((bf16[32,4096]{1,0:T(8,128)(2,1)S(1)}, bf16[32,4096]{1,0:T(8,128)(2,1)}, u32[]{:S(2)}) %copy-start) | copy-done | bytes 262168
  47.3 0.0 copy-start.1
  47.3 0.9 %copy-done.1 = bf16[32,2048]{1,0:T(8,128)(2,1)S(1)} copy-done((bf16[32,2048]{1,0:T(8,128)(2,1)S(1)}, bf16[32,2048]{1,0:T(8,128)(2,1)}, u32[]{:S(2)}) %copy-start.1) | copy-done | bytes 131096
  48.2 12.3 %product.1 = f32[2048,4096]{1,0:T(8,128)} custom-call(bf16[32,2048]{1,0:T(8,128)(2,1)S(1)} %copy-done.1, bf16[32,4096]{1,0:T(8,128)(2,1)S(1)} %copy-done), custom_call_target="tpu_custom_call" | custom-call | tf_op jit(solution)/shard_map/product/pallas_call | solution.py:355
  (3 shorter events, 0.1 us)
Async XLA Ops:
  46.3 1.0 %copy-start = (bf16[32,4096]{1,0:T(8,128)(2,1)S(1)}, bf16[32,4096]{1,0:T(8,128)(2,1)}, u32[]{:S(2)}) copy-start(bf16[32,4096]{1,0:T(8,128)(2,1)} %get-tuple-element.8.owned_ref) | copy-start | bytes 786436
  47.3 0.9 %copy-start.1 = (bf16[32,2048]{1,0:T(8,128)(2,1)S(1)}, bf16[32,2048]{1,0:T(8,128)(2,1)}, u32[]{:S(2)}) copy-start(bf16[32,2048]{1,0:T(8,128)(2,1)} %get-tuple-element.7.rows_ref) | copy-start | bytes 393220

commit v5 on v4

--- a/solution.py
+++ b/solution.py
@@ -346,7 +346,7 @@
             pltpu.SemaphoreType.DMA((ratio, groups)),
         ],
         compiler_params=pltpu.CompilerParams(
-            collective_id=0, has_side_effects=True, vmem_limit_bytes=60 * 2**20
+            collective_id=0, has_side_effects=True, vmem_limit_bytes=119 * 2**19
         ),
         name="gather",
     )(codes, valence_energy, conduction_energy, valence_waves, conduction_waves, first_table, second_table, xtable)

time: 60.8 us -> 60.8 us (level)
  no operation moved by 1% of the time
where the time goes in v5:
time: 60.8 us; the launch traced here: 60.5 us
  Pallas kernels  54.7 us (90%)
  other arithmetic  3.1 us (5%)
  local copies, waits for them, and re-layouts  2.73 us (4%)
    pallas_call x1, Pallas kernels, on_device(): pl.pallas_call(functools.partial(gather_kernel, length, groups, owners, m...  42.3 us
    pallas_call x1, Pallas kernels, on_device(): pl.pallas_call(product_kernel, grid=(own // tile,), out_shape=jax.ShapeDt...  12.3 us
    unnamed x4, local copies, waits for them, and re-layouts  1.85 us
    add x1, other arithmetic, on_device(): codes = (kx + (ky * LANES + comp - imag * length << 8) + (imag << 20))[None]  1.32 us

profile of v5, /device:TPU:24, one launch (start us, length us, event | category | flops | bytes accessed | tf_op | source)
XLA Modules:
  0.0 60.5 jit_solution(18329305582694662676)
XLA Ops:
  0.0 1.3 %fusion.12 = s32[2048]{0:T(1024)} fusion(s32[2048]{0:T(1024)} %param.9), kind=kLoop, calls=%fused_computation.27 | loop fusion | flops 69632 | bytes 16384 | tf_op jit(solution)/shard_map/add | solution.py:313
  1.3 0.2 fusion.10
  1.5 0.2 multiply_convert_fusion
  1.8 0.6 fusion.18.xtable_ref
  2.4 0.6 %fusion.4.first_ref = bf16[96,256]{1,0:T(8,128)(2,1)} fusion(bf16[96,96]{1,0:T(8,128)(2,1)S(1)} %fusion.10, bf16[96,96]{1,0:T(8,128)(2,1)S(1)} %get-tuple-element.12), kind=kLoop, calls=%fused_computation.8 | loop fusion | flops 196608 | bytes 86016 | tf_op jit(solution)/shard_map/concatenate | solution.py:293
  3.0 0.1 maximum_bitcast_fusion
  3.2 0.1 copy.6
  3.3 0.7 %reshape.3.second_ref = bf16[192,192]{1,0:T(8,128)(2,1)} reshape(bf16[96,2,192]{2,1,0:T(2,128)(2,1)S(1)} %copy.6) | data formatting | bytes 147456 | tf_op jit(solution)/shard_map/reshape | solution.py:300
  4.0 42.3 %gather.1 = (bf16[32,2048]{1,0:T(8,128)(2,1)}, bf16[32,4096]{1,0:T(8,128)(2,1)}) custom-call(s32[1,2048]{1,0:T(1,128)} %bitcast.5, f32[2]{0:T(128)} %valence_energy.1, f32[4]{0:T(128)} %conduction_energy.1, bf16[2,12,96,96]{3,2,1,0:T(8,128)(2,1)} %valence_hbm.1, bf16[4,12,96,96]{3,2,1,0:T(8,128)(2,1)} %conduction_hbm.1, bf16[96,256]{1,0:T(8,128)(2,1)} %fusion.4.first_ref, ...), custom_call_target="tpu_custom_call" | custom-call | tf_op jit(solution)/shard_map/gather/pallas_call | solution.py:314
  46.3 0.0 copy-start
  46.4 0.9 %copy-done = bf16[32,4096]{1,0:T(8,128)(2,1)S(1)} copy-done((bf16[32,4096]{1,0:T(8,128)(2,1)S(1)}, bf16[32,4096]{1,0:T(8,128)(2,1)}, u32[]{:S(2)}) %copy-start) | copy-done | bytes 262168
  47.3 0.0 copy-start.1
  47.3 0.9 %copy-done.1 = bf16[32,2048]{1,0:T(8,128)(2,1)S(1)} copy-done((bf16[32,2048]{1,0:T(8,128)(2,1)S(1)}, bf16[32,2048]{1,0:T(8,128)(2,1)}, u32[]{:S(2)}) %copy-start.1) | copy-done | bytes 131096
  48.2 12.3 %product.1 = f32[2048,4096]{1,0:T(8,128)} custom-call(bf16[32,2048]{1,0:T(8,128)(2,1)S(1)} %copy-done.1, bf16[32,4096]{1,0:T(8,128)(2,1)S(1)} %copy-done), custom_call_target="tpu_custom_call" | custom-call | tf_op jit(solution)/shard_map/product/pallas_call | solution.py:355
  (3 shorter events, 0.1 us)
Async XLA Ops:
  46.3 1.0 %copy-start = (bf16[32,4096]{1,0:T(8,128)(2,1)S(1)}, bf16[32,4096]{1,0:T(8,128)(2,1)}, u32[]{:S(2)}) copy-start(bf16[32,4096]{1,0:T(8,128)(2,1)} %get-tuple-element.8.owned_ref) | copy-start | bytes 786436
  47.3 0.9 %copy-start.1 = (bf16[32,2048]{1,0:T(8,128)(2,1)S(1)}, bf16[32,2048]{1,0:T(8,128)(2,1)}, u32[]{:S(2)}) copy-start(bf16[32,2048]{1,0:T(8,128)(2,1)} %get-tuple-element.7.rows_ref) | copy-start | bytes 393220
